TPU v7x, 32 devices: a whole 2x2x4 slice. The times are simulated.
32 devices in a mesh: row: 4 (over y, core), col: 8 (over z, x).
Axes of the slice: x: 2, y: 2, z: 4, core: 2. Of those that a mesh axis runs over, the one named last changes fastest.
Arguments:
- objects: float32 [2, 2, 1024, 2048], P(None, None, 'row', 'col'), may hold values from -5 to 5
- probe: float32 [2, 2, 128, 128], replicated, may hold values from -6 to 6
- amplitudes: bfloat16 [4, 8, 6, 128, 128], P('row', 'col'), may hold values from 0.29882812 to 3
- owners: int32 [4, 8, 6], P('row', 'col'), may hold values from 0 to 7, as said below
- off_rows: int32 [4, 8, 6], P('row', 'col'), may hold values from 0 to 256
- off_cols: int32 [4, 8, 6], P('row', 'col'), may hold values from 0 to 256
Outputs:
- gradient: float32 [2, 2, 1024, 2048], P(None, None, 'row', 'col')
Inputs may be any that keep to these rules, and one draw needn't show every extreme that they name: Each device's 6 positions go to owners of its own tile row whose tile column is the device's own plus one of -3, -2, -1, 1, 2, 3, 4, taken modulo 8; at most 2 of them to one owner, exactly 2 to one owner from some device of every tile row. Over all devices of a tile row, one owner receives exactly 12 positions and every other owner at most 7.
All inputs are finite; a program needn't handle non-finite values.
Results may differ from a plain program's by a relative error of at most 0.009.
Values may be sent and summed in bfloat16 or wider, within the bound.
No kernel may reach another device: no remote copies, remote signals or barrier semaphores. Data moves between devices by JAX's collectives and lax.ppermute only.
A program may use at most 64 MiB of HBM per device.

v0:
```python
import math

import jax
import jax.numpy as jnp
from jax import lax
from jax.sharding import PartitionSpec as P

CAP = 2
RMAX = 12


FRESNEL = 24.0
REACH_OFFSETS = (-3, -2, -1, 1, 2, 3, 4)


def shifted(block, axis, distance):
    devices = range(lax.axis_size(axis))
    route = [((i - distance) % len(devices), i) for i in devices]
    return lax.ppermute(block, axis, route)


def padded(array, sides, width):
    for axis, dim in sides:
        size, length = (lax.axis_size(axis), array.shape[dim])
        up = [(i, (i + 1) % size) for i in range(size - 1)]
        down = [(j, i) for i, j in up]
        last = lax.slice_in_dim(array, length - width, length, axis=dim)
        first = lax.slice_in_dim(array, 0, width, axis=dim)
        before = lax.ppermute(last, axis, up)
        after = lax.ppermute(first, axis, down)
        array = jnp.concatenate([before, array, after], axis=dim)
    return array


def make_mats(width):
    idx = jnp.arange(width, dtype=jnp.int32)
    prod = idx[:, None] * idx[None, :] % width
    angle = prod.astype(jnp.float32) * (2.0 * math.pi / width)
    scale = 1.0 / math.sqrt(width)
    f_re = jnp.cos(angle) * scale
    f_im = -jnp.sin(angle) * scale
    centred = (idx + width // 2) % width - width // 2
    theta = (centred * centred).astype(jnp.float32) * (math.pi * FRESNEL / (width * width))
    d_re = jnp.cos(theta)
    d_im = -jnp.sin(theta)
    m_re = d_re[:, None] * f_re - d_im[:, None] * f_im
    m_im = d_re[:, None] * f_im + d_im[:, None] * f_re
    high = lax.Precision.HIGHEST
    k_re = jnp.dot(f_re, m_re, precision=high) + jnp.dot(f_im, m_im, precision=high)
    k_im = jnp.dot(f_re, m_im, precision=high) - jnp.dot(f_im, m_re, precision=high)
    f_re = f_re.astype(jnp.bfloat16)
    f_im = f_im.astype(jnp.bfloat16)
    k_re = k_re.astype(jnp.bfloat16)
    k_im = k_im.astype(jnp.bfloat16)

    def left_stack(a_re, a_im):
        return jnp.stack([jnp.stack([a_re, -a_im]), jnp.stack([a_im, a_re])])

    def right_stack(a_re, a_im):
        return jnp.stack([jnp.stack([a_re, a_im]), jnp.stack([-a_im, a_re])])

    return (
        left_stack(k_re, k_im),
        right_stack(k_re, k_im),
        left_stack(f_re, f_im),
        right_stack(f_re, f_im),
        left_stack(k_re, -k_im),
        right_stack(k_re, -k_im),
        left_stack(f_re, -f_im),
        right_stack(f_re, -f_im),
    )


def apply_left(table, field):
    return jnp.einsum("trpq,nrqs->ntps", table, field, preferred_element_type=jnp.float32)


def apply_right(field, table):
    return jnp.einsum("nrpq,rtqs->ntps", field, table, preferred_element_type=jnp.float32)


def cmul(first, second):
    a_re = first[..., 0, :, :]
    a_im = first[..., 1, :, :]
    b_re = second[..., 0, :, :]
    b_im = second[..., 1, :, :]
    return jnp.stack([a_re * b_re - a_im * b_im, a_re * b_im + a_im * b_re], axis=-3)


def conj(field):
    return jnp.stack([field[..., 0, :, :], -field[..., 1, :, :]], axis=-3)


def pattern_grad(window, probe, amp, valid, mats):
    k_left, k_right, f_left, f_right, kc_left, kc_right, fc_left, fc_right = mats
    psi_one = cmul(probe, window[0]).astype(jnp.bfloat16)
    upper = apply_left(k_left, psi_one).astype(jnp.bfloat16)
    phi = apply_right(upper, k_right)
    psi_two = cmul(phi, window[1]).astype(jnp.bfloat16)
    vfield = apply_left(f_left, psi_two).astype(jnp.bfloat16)
    far = apply_right(vfield, f_right)
    inten = jnp.sum(far * far, axis=(0, 1))
    ratio = amp.astype(jnp.float32) / jnp.maximum(jnp.sqrt(inten), 1.0)
    resid = (far * (valid * (1.0 - ratio))).astype(jnp.bfloat16)
    wfield = apply_left(fc_left, resid).astype(jnp.bfloat16)
    g_two = apply_right(wfield, fc_right)
    g_phi = cmul(conj(window[1]), g_two).astype(jnp.bfloat16)
    yfield = apply_left(kc_left, g_phi).astype(jnp.bfloat16)
    g_one = apply_right(yfield, kc_right)
    grad_one = jnp.sum(cmul(conj(probe), g_one), axis=0)
    grad_two = jnp.sum(cmul(conj(phi), g_two), axis=0)
    return jnp.stack([grad_one, grad_two])


def pad_axis(piece, axis, before, after):
    widths = [(0, 0)] * piece.ndim
    widths[axis] = (before, after)
    return jnp.pad(piece, widths)


def fold_bands(wide, border, rows, cols):
    top = wide[:, :, :border]
    middle = wide[:, :, 2 * border : 2 * border + rows]
    bottom = wide[:, :, rows + 3 * border :]
    folded = middle + pad_axis(top, 2, 0, rows - border) + pad_axis(bottom, 2, rows - border, 0)
    left = folded[:, :, :, :border]
    centre = folded[:, :, :, 2 * border : 2 * border + cols]
    right = folded[:, :, :, cols + 3 * border :]
    return centre + pad_axis(left, 3, 0, cols - border) + pad_axis(right, 3, cols - border, 0)


def local(objects, probe, amplitudes, owners, off_rows, off_cols):
    width = amplitudes.shape[-1]
    border = width // 2
    count = amplitudes.shape[2]
    kinds = len(REACH_OFFSETS)
    slots = CAP * kinds
    ncols = lax.axis_size("col")
    myself = lax.axis_index("col")
    rows = objects.shape[2]
    cols = objects.shape[3]
    mats = make_mats(width)
    dest = owners.reshape(count)
    rows_at = off_rows.reshape(count)
    cols_at = off_cols.reshape(count)
    apart = (dest - myself) % ncols
    kind_of = jnp.zeros_like(dest)
    for number, offset in enumerate(REACH_OFFSETS):
        kind_of = kind_of + number * (apart == offset % ncols).astype(jnp.int32)
    series = jnp.arange(count, dtype=jnp.int32)
    before = (dest[:, None] == dest[None, :]) & (series[None, :] < series[:, None])
    rank = jnp.sum(before.astype(jnp.int32), axis=1)
    target = kind_of * CAP + rank
    choose = jnp.arange(slots, dtype=jnp.int32)[:, None] == target[None, :]
    flat = amplitudes.reshape(count, width * width)
    sent = jnp.dot(choose.astype(jnp.bfloat16), flat, preferred_element_type=jnp.float32).astype(
        jnp.bfloat16
    )
    details = jnp.stack([rows_at, cols_at, jnp.ones_like(rows_at)], axis=1)
    sent_details = jnp.sum(choose.astype(jnp.int32)[:, :, None] * details[None, :, :], axis=1)
    got_amps = []
    got_details = []
    for number, offset in enumerate(REACH_OFFSETS):
        piece = sent[number * CAP : (number + 1) * CAP]
        piece_details = sent_details[number * CAP : (number + 1) * CAP]
        came, came_details = shifted((piece, piece_details), "col", offset)
        got_amps.append(came)
        got_details.append(came_details)
    arrived = jnp.concatenate(got_amps, axis=0)
    arrived_details = jnp.concatenate(got_details, axis=0)
    live = arrived_details[:, 2]
    place = jnp.cumsum(live) - live
    pick = (place[None, :] == jnp.arange(RMAX, dtype=jnp.int32)[:, None]) & (live[None, :] > 0)
    held = jnp.dot(pick.astype(jnp.bfloat16), arrived, preferred_element_type=jnp.float32)
    held = held.astype(jnp.bfloat16).reshape(RMAX, width, width)
    held_details = jnp.sum(pick.astype(jnp.int32)[:, :, None] * arrived_details[None, :, :], axis=1)
    extended = padded(objects, (("row", 2), ("col", 3)), border)

    def visit(carry, item):
        amp, detail = item
        zero = jnp.zeros((), jnp.int32)
        corner = (zero, zero, detail[0], detail[1])
        window = lax.dynamic_slice(extended, corner, (objects.shape[0], 2, width, width))
        valid = detail[2].astype(jnp.float32)
        grads = pattern_grad(window, probe, amp, valid, mats)
        current = lax.dynamic_slice(carry, corner, grads.shape)
        return (lax.dynamic_update_slice(carry, current + grads, corner), None)

    summed, _ = lax.scan(visit, jnp.zeros(extended.shape, jnp.float32), (held, held_details))
    wide = padded(summed, (("row", 2), ("col", 3)), border)
    result = fold_bands(wide, border, rows, cols)
    return result


def solution(mesh):
    placed = (
        P(None, None, "row", "col"),
        P(),
        P("row", "col", None, None, None),
        P("row", "col", None),
        P("row", "col", None),
        P("row", "col", None),
    )
    return jax.shard_map(
        local, mesh=mesh, in_specs=placed, out_specs=P(None, None, "row", "col"), check_vma=False
    )
```

profile of v0, /device:TPU:8, one launch (start us, length us, event | category | flops | bytes accessed | tf_op | source)
XLA Modules:
  0.0 437.8 jit_solution(15998610888696377432)
XLA Ops:
  3.2 2.6 collective-permute-start.6
  17.1 3.0 collective-permute-start.1
  21.2 3.8 collective-permute-start.16
  31.4 3.1 collective-permute-done.8
  35.8 1.9 collective-permute-start.9
  37.7 4.8 %collective-permute-start.10 = (f32[2,2,384,64]{2,3,1,0:T(8,128)}, f32[2,2,384,64]{2,3,1,0:T(8,128)}, u32[]{:S(2)}, u32[]{:S(2)}) collective-permute-start(f32[2,2,384,64]{2,3,1,0:T(8,128)} %get-tuple-element.280), channel_id=1, source_target_pairs={{1,0},{2,1},{3,2},{4,3},{5,4},{6,5},{7,6},{9,8},{10,9},{11,10},{12... | collective-permute-start | bytes 1179656 | tf_op jit(solution)/shard_map/ppermute | solution.py:30
  42.6 3.1 collective-permute-start.12
  46.7 12.5 %collective-permute-done.13 = bf16[2,16384]{1,0:T(2,128)(2,1)S(1)} collective-permute-done((bf16[2,16384]{1,0:T(2,128)(2,1)}, bf16[2,16384]{1,0:T(2,128)(2,1)S(1)}, u32[]{:S(2)}, u32[]{:S(2)}) %collective-permute-start.13) | collective-permute-done | bytes 65568 | tf_op jit(solution)/shard_map/ppermute | solution.py:19
  59.2 3.5 concatenate.21
  65.0 3.1 pad_maximum_fusion.1
  68.3 310.9 %while.12 = (s32[]{:T(128)}, f32[2,2,384,384]{2,3,1,0:T(8,128)S(1)}, s32[12,3]{1,0:T(8,128)S(1)}, f32[2,2,128,128]{2,3,1,0:T(8,128)S(1)}, f32[2,2,384,384]{2,3,1...) while((s32[]{:T(128)}, ...), condition=%wide.region_8.9_spmd, body=%wide.region_4.8_spmd.sunk | while | flops 271368192 | bytes 12681745 | solution.py:189
  80.9 2.0 multiply_reduce_fusion.4
  85.8 1.6 subtract_convert_fusion.8
  91.7 3.4 dynamic_update_slice.6
  107.8 2.0 multiply_reduce_fusion.4
  112.7 1.6 subtract_convert_fusion.8
  118.6 3.4 dynamic_update_slice.6
  134.7 2.0 multiply_reduce_fusion.4
  139.6 1.6 subtract_convert_fusion.8
  145.4 3.0 dynamic_update_slice.6
  161.2 2.0 multiply_reduce_fusion.4
  166.1 1.6 subtract_convert_fusion.8
  171.9 3.4 dynamic_update_slice.6
  188.0 2.0 multiply_reduce_fusion.4
  198.8 3.2 dynamic_update_slice.6
  214.7 2.0 multiply_reduce_fusion.4
  225.5 1.8 dynamic_update_slice.6
  240.0 2.0 multiply_reduce_fusion.4
  250.8 1.8 dynamic_update_slice.6
  265.3 2.0 multiply_reduce_fusion.4
  276.1 1.8 dynamic_update_slice.6
  290.6 2.0 multiply_reduce_fusion.4
  301.4 1.8 dynamic_update_slice.6
  315.9 2.0 multiply_reduce_fusion.4
  326.7 1.8 dynamic_update_slice.6
  341.2 2.0 multiply_reduce_fusion.4
  346.1 1.6 subtract_convert_fusion.8
  352.0 1.8 dynamic_update_slice.6
  366.5 2.0 multiply_reduce_fusion.4
  371.4 1.6 subtract_convert_fusion.8
  377.3 1.8 dynamic_update_slice.6
  379.2 2.0 copy.138
  382.3 16.1 %collective-permute-start.18 = (f32[2,2,64,384]{3,2,1,0:T(8,128)S(1)}, f32[2,2,64,384]{3,2,1,0:T(8,128)}, u32[]{:S(2)}, u32[]{:S(2)}) collective-permute-start(f32[2,2,64,384]{3,2,1,0:T(8,128)S(1)} %get-tuple-element.277), channel_id=1, source_target_pairs={{0,8},{8,16},{16,24},{1,9},{9,17},{17,25},{2,10},{10,18},{18,26},{... | collective-permute-start | bytes 1179656 | tf_op jit(solution)/shard_map/ppermute | solution.py:29
  402.2 2.1 copy.141
  405.8 1.9 collective-permute-start.20
  407.7 4.8 %collective-permute-start.21 = (f32[2,2,512,64]{2,3,1,0:T(8,128)S(1)}, f32[2,2,512,64]{2,3,1,0:T(8,128)S(1)}, u32[]{:S(2)}, u32[]{:S(2)}) collective-permute-start(f32[2,2,512,64]{2,3,1,0:T(8,128)S(1)} %get-tuple-element.276), channel_id=1, source_target_pairs={{1,0},{2,1},{3,2},{4,3},{5,4},{6,5},{7,6},{9,8},{10,9},{11,10},{12... | collective-permute-start | bytes 1572872 | tf_op jit(solution)/shard_map/ppermute | solution.py:30
  412.5 12.4 %collective-permute-done.20 = f32[2,2,512,64]{2,3,1,0:T(8,128)S(1)} collective-permute-done((f32[2,2,512,64]{2,3,1,0:T(8,128)S(1)}, f32[2,2,512,64]{2,3,1,0:T(8,128)S(1)}, u32[]{:S(2)}, u32[]{:S(2)}) %collective-permute-start.20) | collective-permute-done | bytes 524320 | tf_op jit(solution)/shard_map/ppermute | solution.py:29
  424.9 9.6 %collective-permute-done.21 = f32[2,2,512,64]{2,3,1,0:T(8,128)S(1)} collective-permute-done((f32[2,2,512,64]{2,3,1,0:T(8,128)S(1)}, f32[2,2,512,64]{2,3,1,0:T(8,128)S(1)}, u32[]{:S(2)}, u32[]{:S(2)}) %collective-permute-start.21) | collective-permute-done | bytes 524320 | tf_op jit(solution)/shard_map/ppermute | solution.py:30
  (485 shorter events, 227.7 us)
Async XLA Ops:
  3.2 13.8 %collective-permute-start.6 = (s32[2,3]{0,1:T(4,128)}, s32[2,3]{0,1:T(4,128)}, u32[]{:S(2)}, u32[]{:S(2)}) collective-permute-start(s32[2,3]{0,1:T(4,128)} %get-tuple-element.302), channel_id=1, source_target_pairs={{4,0},{5,1},{6,2},{7,3},{0,4},{1,5},{2,6},{3,7},{12,8},{13,9},{14,... | collective-permute-start | bytes 80 | tf_op jit(solution)/shard_map/ppermute | solution.py:19
  5.8 14.3 %collective-permute-start.5 = (s32[2,3]{0,1:T(4,128)}, s32[2,3]{0,1:T(4,128)}, u32[]{:S(2)}, u32[]{:S(2)}) collective-permute-start(s32[2,3]{0,1:T(4,128)} %get-tuple-element.303), channel_id=1, source_target_pairs={{5,0},{6,1},{7,2},{0,3},{1,4},{2,5},{3,6},{4,7},{13,8},{14,9},{15,... | collective-permute-start | bytes 80 | tf_op jit(solution)/shard_map/ppermute | solution.py:19
  6.1 14.6 %collective-permute-start.4 = (s32[2,3]{0,1:T(4,128)}, s32[2,3]{0,1:T(4,128)}, u32[]{:S(2)}, u32[]{:S(2)}) collective-permute-start(s32[2,3]{0,1:T(4,128)} %get-tuple-element.304), channel_id=1, source_target_pairs={{6,0},{7,1},{0,2},{1,3},{2,4},{3,5},{4,6},{5,7},{14,8},{15,9},{8,1... | collective-permute-start | bytes 80 | tf_op jit(solution)/shard_map/ppermute | solution.py:19
  7.7 13.5 %collective-permute-start.3 = (s32[2,3]{0,1:T(4,128)S(1)}, s32[2,3]{0,1:T(4,128)}, u32[]{:S(2)}, u32[]{:S(2)}) collective-permute-start(s32[2,3]{0,1:T(4,128)S(1)} %get-tuple-element.305), channel_id=1, source_target_pairs={{7,0},{0,1},{1,2},{2,3},{3,4},{4,5},{5,6},{6,7},{15,8},{8,9},{9,10... | collective-permute-start | bytes 80 | tf_op jit(solution)/shard_map/ppermute | solution.py:19
  9.2 15.7 %collective-permute-start.2 = (s32[2,3]{0,1:T(4,128)S(1)}, s32[2,3]{0,1:T(4,128)}, u32[]{:S(2)}, u32[]{:S(2)}) collective-permute-start(s32[2,3]{0,1:T(4,128)S(1)} %get-tuple-element.306), channel_id=1, source_target_pairs={{1,0},{2,1},{3,2},{4,3},{5,4},{6,5},{7,6},{0,7},{9,8},{10,9},{11,1... | collective-permute-start | bytes 80 | tf_op jit(solution)/shard_map/ppermute | solution.py:19
  17.1 9.4 %collective-permute-start.1 = (s32[2,3]{0,1:T(4,128)S(1)}, s32[2,3]{0,1:T(4,128)S(1)}, u32[]{:S(2)}, u32[]{:S(2)}) collective-permute-start(s32[2,3]{0,1:T(4,128)S(1)} %get-tuple-element.307), channel_id=1, source_target_pairs={{2,0},{3,1},{4,2},{5,3},{6,4},{7,5},{0,6},{1,7},{10,8},{11,9},{12,... | collective-permute-start | bytes 80 | tf_op jit(solution)/shard_map/ppermute | solution.py:19
  20.1 8.3 %collective-permute-start = (s32[2,3]{0,1:T(4,128)S(1)}, s32[2,3]{0,1:T(4,128)S(1)}, u32[]{:S(2)}, u32[]{:S(2)}) collective-permute-start(s32[2,3]{0,1:T(4,128)S(1)} %get-tuple-element.308), channel_id=1, source_target_pairs={{3,0},{4,1},{5,2},{6,3},{7,4},{0,5},{1,6},{2,7},{11,8},{12,9},{13,... | collective-permute-start | bytes 80 | tf_op jit(solution)/shard_map/ppermute | solution.py:19
  20.6 17.1 %collective-permute-start.17 = (bf16[2,16384]{1,0:T(2,128)(2,1)}, bf16[2,16384]{1,0:T(2,128)(2,1)S(1)}, u32[]{:S(2)}, u32[]{:S(2)}) collective-permute-start(bf16[2,16384]{1,0:T(2,128)(2,1)} %get-tuple-element.283), channel_id=1, source_target_pairs={{4,0},{5,1},{6,2},{7,3},{0,4},{1,5},{2,6},{3,7},{12,8},{13,9},{14,... | collective-permute-start | bytes 196616 | tf_op jit(solution)/shard_map/ppermute | solution.py:19
  21.2 21.4 %collective-permute-start.16 = (bf16[2,16384]{1,0:T(2,128)(2,1)}, bf16[2,16384]{1,0:T(2,128)(2,1)S(1)}, u32[]{:S(2)}, u32[]{:S(2)}) collective-permute-start(bf16[2,16384]{1,0:T(2,128)(2,1)} %get-tuple-element.284), channel_id=1, source_target_pairs={{5,0},{6,1},{7,2},{0,3},{1,4},{2,5},{3,6},{4,7},{13,8},{14,9},{15,... | collective-permute-start | bytes 196616 | tf_op jit(solution)/shard_map/ppermute | solution.py:19
  24.9 17.7 %collective-permute-start.15 = (bf16[2,16384]{1,0:T(2,128)(2,1)}, bf16[2,16384]{1,0:T(2,128)(2,1)}, u32[]{:S(2)}, u32[]{:S(2)}) collective-permute-start(bf16[2,16384]{1,0:T(2,128)(2,1)} %get-tuple-element.285), channel_id=1, source_target_pairs={{6,0},{7,1},{0,2},{1,3},{2,4},{3,5},{4,6},{5,7},{14,8},{15,9},{8,1... | collective-permute-start | bytes 196616 | tf_op jit(solution)/shard_map/ppermute | solution.py:19
  27.1 4.2 collective-permute-start.7
  29.0 5.5 %collective-permute-start.8 = (f32[2,2,64,256]{2,3,1,0:T(8,128)S(1)}, f32[2,2,64,256]{2,3,1,0:T(8,128)S(1)}, u32[]{:S(2)}, u32[]{:S(2)}) collective-permute-start(f32[2,2,64,256]{2,3,1,0:T(8,128)S(1)} %get-tuple-element.282), channel_id=1, source_target_pairs={{8,0},{16,8},{24,16},{9,1},{17,9},{25,17},{10,2},{18,10},{26,18},{... | collective-permute-start | bytes 786440 | tf_op jit(solution)/shard_map/ppermute | solution.py:30
  31.3 14.5 %collective-permute-start.14 = (bf16[2,16384]{1,0:T(2,128)(2,1)}, bf16[2,16384]{1,0:T(2,128)(2,1)}, u32[]{:S(2)}, u32[]{:S(2)}) collective-permute-start(bf16[2,16384]{1,0:T(2,128)(2,1)} %get-tuple-element.286), channel_id=1, source_target_pairs={{7,0},{0,1},{1,2},{2,3},{3,4},{4,5},{5,6},{6,7},{15,8},{8,9},{9,10... | collective-permute-start | bytes 196616 | tf_op jit(solution)/shard_map/ppermute | solution.py:19
  35.8 29.2 %collective-permute-start.9 = (f32[2,2,384,64]{2,3,1,0:T(8,128)}, f32[2,2,384,64]{2,3,1,0:T(8,128)}, u32[]{:S(2)}, u32[]{:S(2)}) collective-permute-start(f32[2,2,384,64]{2,3,1,0:T(8,128)} %get-tuple-element.279), channel_id=1, source_target_pairs={{0,1},{1,2},{2,3},{3,4},{4,5},{5,6},{6,7},{8,9},{9,10},{10,11},{11... | collective-permute-start | bytes 1179656 | tf_op jit(solution)/shard_map/ppermute | solution.py:29
  37.7 27.2 %collective-permute-start.10 = (f32[2,2,384,64]{2,3,1,0:T(8,128)}, f32[2,2,384,64]{2,3,1,0:T(8,128)}, u32[]{:S(2)}, u32[]{:S(2)}) collective-permute-start(f32[2,2,384,64]{2,3,1,0:T(8,128)} %get-tuple-element.280), channel_id=1, source_target_pairs={{1,0},{2,1},{3,2},{4,3},{5,4},{6,5},{7,6},{9,8},{10,9},{11,10},{12... | collective-permute-start | bytes 1179656 | tf_op jit(solution)/shard_map/ppermute | solution.py:30
  42.6 16.7 %collective-permute-start.13 = (bf16[2,16384]{1,0:T(2,128)(2,1)}, bf16[2,16384]{1,0:T(2,128)(2,1)S(1)}, u32[]{:S(2)}, u32[]{:S(2)}) collective-permute-start(bf16[2,16384]{1,0:T(2,128)(2,1)} %get-tuple-element.287), channel_id=1, source_target_pairs={{1,0},{2,1},{3,2},{4,3},{5,4},{6,5},{7,6},{0,7},{9,8},{10,9},{11,1... | collective-permute-start | bytes 196616 | tf_op jit(solution)/shard_map/ppermute | solution.py:19
  42.6 16.6 %collective-permute-start.12 = (bf16[2,16384]{1,0:T(2,128)(2,1)}, bf16[2,16384]{1,0:T(2,128)(2,1)S(1)}, u32[]{:S(2)}, u32[]{:S(2)}) collective-permute-start(bf16[2,16384]{1,0:T(2,128)(2,1)} %get-tuple-element.288), channel_id=1, source_target_pairs={{2,0},{3,1},{4,2},{5,3},{6,4},{7,5},{0,6},{1,7},{10,8},{11,9},{12,... | collective-permute-start | bytes 196616 | tf_op jit(solution)/shard_map/ppermute | solution.py:19
  45.8 13.4 %collective-permute-start.11 = (bf16[2,16384]{1,0:T(2,128)(2,1)}, bf16[2,16384]{1,0:T(2,128)(2,1)S(1)}, u32[]{:S(2)}, u32[]{:S(2)}) collective-permute-start(bf16[2,16384]{1,0:T(2,128)(2,1)} %get-tuple-element.289), channel_id=1, source_target_pairs={{3,0},{4,1},{5,2},{6,3},{7,4},{0,5},{1,6},{2,7},{11,8},{12,9},{13,... | collective-permute-start | bytes 196616 | tf_op jit(solution)/shard_map/ppermute | solution.py:19
  68.3 14.6 %copy-start.2 = (bf16[2,2,128,128]{3,2,0,1:T(8,128)(2,1)}, bf16[2,2,128,128]{3,2,0,1:T(8,128)(2,1)S(1)}, u32[]{:S(2)}) copy-start(bf16[2,2,128,128]{3,2,0,1:T(8,128)(2,1)S(1)} %get-tuple-element.457) | copy-start | bytes 393220 | tf_op jit(solution)/shard_map/while
  68.3 14.6 %copy-start.4 = (bf16[2,2,128,128]{3,2,1,0:T(8,128)(2,1)}, bf16[2,2,128,128]{3,2,1,0:T(8,128)(2,1)S(1)}, u32[]{:S(2)}) copy-start(bf16[2,2,128,128]{3,2,1,0:T(8,128)(2,1)S(1)} %get-tuple-element.458) | copy-start | bytes 393220 | tf_op jit(solution)/shard_map/while
  95.2 14.6 %copy-start.2 = (bf16[2,2,128,128]{3,2,0,1:T(8,128)(2,1)}, bf16[2,2,128,128]{3,2,0,1:T(8,128)(2,1)S(1)}, u32[]{:S(2)}) copy-start(bf16[2,2,128,128]{3,2,0,1:T(8,128)(2,1)S(1)} %get-tuple-element.457) | copy-start | bytes 393220 | tf_op jit(solution)/shard_map/while
  95.2 14.6 %copy-start.4 = (bf16[2,2,128,128]{3,2,1,0:T(8,128)(2,1)}, bf16[2,2,128,128]{3,2,1,0:T(8,128)(2,1)S(1)}, u32[]{:S(2)}) copy-start(bf16[2,2,128,128]{3,2,1,0:T(8,128)(2,1)S(1)} %get-tuple-element.458) | copy-start | bytes 393220 | tf_op jit(solution)/shard_map/while
  122.0 14.6 %copy-start.2 = (bf16[2,2,128,128]{3,2,0,1:T(8,128)(2,1)}, bf16[2,2,128,128]{3,2,0,1:T(8,128)(2,1)S(1)}, u32[]{:S(2)}) copy-start(bf16[2,2,128,128]{3,2,0,1:T(8,128)(2,1)S(1)} %get-tuple-element.457) | copy-start | bytes 393220 | tf_op jit(solution)/shard_map/while
  122.0 14.6 %copy-start.4 = (bf16[2,2,128,128]{3,2,1,0:T(8,128)(2,1)}, bf16[2,2,128,128]{3,2,1,0:T(8,128)(2,1)S(1)}, u32[]{:S(2)}) copy-start(bf16[2,2,128,128]{3,2,1,0:T(8,128)(2,1)S(1)} %get-tuple-element.458) | copy-start | bytes 393220 | tf_op jit(solution)/shard_map/while
  148.5 14.6 %copy-start.2 = (bf16[2,2,128,128]{3,2,0,1:T(8,128)(2,1)}, bf16[2,2,128,128]{3,2,0,1:T(8,128)(2,1)S(1)}, u32[]{:S(2)}) copy-start(bf16[2,2,128,128]{3,2,0,1:T(8,128)(2,1)S(1)} %get-tuple-element.457) | copy-start | bytes 393220 | tf_op jit(solution)/shard_map/while
  148.5 14.6 %copy-start.4 = (bf16[2,2,128,128]{3,2,1,0:T(8,128)(2,1)}, bf16[2,2,128,128]{3,2,1,0:T(8,128)(2,1)S(1)}, u32[]{:S(2)}) copy-start(bf16[2,2,128,128]{3,2,1,0:T(8,128)(2,1)S(1)} %get-tuple-element.458) | copy-start | bytes 393220 | tf_op jit(solution)/shard_map/while
  175.4 14.6 %copy-start.2 = (bf16[2,2,128,128]{3,2,0,1:T(8,128)(2,1)}, bf16[2,2,128,128]{3,2,0,1:T(8,128)(2,1)S(1)}, u32[]{:S(2)}) copy-start(bf16[2,2,128,128]{3,2,0,1:T(8,128)(2,1)S(1)} %get-tuple-element.457) | copy-start | bytes 393220 | tf_op jit(solution)/shard_map/while
  175.4 14.6 %copy-start.4 = (bf16[2,2,128,128]{3,2,1,0:T(8,128)(2,1)}, bf16[2,2,128,128]{3,2,1,0:T(8,128)(2,1)S(1)}, u32[]{:S(2)}) copy-start(bf16[2,2,128,128]{3,2,1,0:T(8,128)(2,1)S(1)} %get-tuple-element.458) | copy-start | bytes 393220 | tf_op jit(solution)/shard_map/while
  202.1 14.6 %copy-start.2 = (bf16[2,2,128,128]{3,2,0,1:T(8,128)(2,1)}, bf16[2,2,128,128]{3,2,0,1:T(8,128)(2,1)S(1)}, u32[]{:S(2)}) copy-start(bf16[2,2,128,128]{3,2,0,1:T(8,128)(2,1)S(1)} %get-tuple-element.457) | copy-start | bytes 393220 | tf_op jit(solution)/shard_map/while
  202.1 14.6 %copy-start.4 = (bf16[2,2,128,128]{3,2,1,0:T(8,128)(2,1)}, bf16[2,2,128,128]{3,2,1,0:T(8,128)(2,1)S(1)}, u32[]{:S(2)}) copy-start(bf16[2,2,128,128]{3,2,1,0:T(8,128)(2,1)S(1)} %get-tuple-element.458) | copy-start | bytes 393220 | tf_op jit(solution)/shard_map/while
  227.4 14.6 %copy-start.2 = (bf16[2,2,128,128]{3,2,0,1:T(8,128)(2,1)}, bf16[2,2,128,128]{3,2,0,1:T(8,128)(2,1)S(1)}, u32[]{:S(2)}) copy-start(bf16[2,2,128,128]{3,2,0,1:T(8,128)(2,1)S(1)} %get-tuple-element.457) | copy-start | bytes 393220 | tf_op jit(solution)/shard_map/while
  227.4 14.6 %copy-start.4 = (bf16[2,2,128,128]{3,2,1,0:T(8,128)(2,1)}, bf16[2,2,128,128]{3,2,1,0:T(8,128)(2,1)S(1)}, u32[]{:S(2)}) copy-start(bf16[2,2,128,128]{3,2,1,0:T(8,128)(2,1)S(1)} %get-tuple-element.458) | copy-start | bytes 393220 | tf_op jit(solution)/shard_map/while
  252.7 14.6 %copy-start.2 = (bf16[2,2,128,128]{3,2,0,1:T(8,128)(2,1)}, bf16[2,2,128,128]{3,2,0,1:T(8,128)(2,1)S(1)}, u32[]{:S(2)}) copy-start(bf16[2,2,128,128]{3,2,0,1:T(8,128)(2,1)S(1)} %get-tuple-element.457) | copy-start | bytes 393220 | tf_op jit(solution)/shard_map/while
  252.7 14.6 %copy-start.4 = (bf16[2,2,128,128]{3,2,1,0:T(8,128)(2,1)}, bf16[2,2,128,128]{3,2,1,0:T(8,128)(2,1)S(1)}, u32[]{:S(2)}) copy-start(bf16[2,2,128,128]{3,2,1,0:T(8,128)(2,1)S(1)} %get-tuple-element.458) | copy-start | bytes 393220 | tf_op jit(solution)/shard_map/while
  278.0 14.6 %copy-start.2 = (bf16[2,2,128,128]{3,2,0,1:T(8,128)(2,1)}, bf16[2,2,128,128]{3,2,0,1:T(8,128)(2,1)S(1)}, u32[]{:S(2)}) copy-start(bf16[2,2,128,128]{3,2,0,1:T(8,128)(2,1)S(1)} %get-tuple-element.457) | copy-start | bytes 393220 | tf_op jit(solution)/shard_map/while
  278.0 14.6 %copy-start.4 = (bf16[2,2,128,128]{3,2,1,0:T(8,128)(2,1)}, bf16[2,2,128,128]{3,2,1,0:T(8,128)(2,1)S(1)}, u32[]{:S(2)}) copy-start(bf16[2,2,128,128]{3,2,1,0:T(8,128)(2,1)S(1)} %get-tuple-element.458) | copy-start | bytes 393220 | tf_op jit(solution)/shard_map/while
  303.3 14.6 %copy-start.2 = (bf16[2,2,128,128]{3,2,0,1:T(8,128)(2,1)}, bf16[2,2,128,128]{3,2,0,1:T(8,128)(2,1)S(1)}, u32[]{:S(2)}) copy-start(bf16[2,2,128,128]{3,2,0,1:T(8,128)(2,1)S(1)} %get-tuple-element.457) | copy-start | bytes 393220 | tf_op jit(solution)/shard_map/while
  303.3 14.6 %copy-start.4 = (bf16[2,2,128,128]{3,2,1,0:T(8,128)(2,1)}, bf16[2,2,128,128]{3,2,1,0:T(8,128)(2,1)S(1)}, u32[]{:S(2)}) copy-start(bf16[2,2,128,128]{3,2,1,0:T(8,128)(2,1)S(1)} %get-tuple-element.458) | copy-start | bytes 393220 | tf_op jit(solution)/shard_map/while
  328.6 14.6 %copy-start.2 = (bf16[2,2,128,128]{3,2,0,1:T(8,128)(2,1)}, bf16[2,2,128,128]{3,2,0,1:T(8,128)(2,1)S(1)}, u32[]{:S(2)}) copy-start(bf16[2,2,128,128]{3,2,0,1:T(8,128)(2,1)S(1)} %get-tuple-element.457) | copy-start | bytes 393220 | tf_op jit(solution)/shard_map/while
  328.6 14.6 %copy-start.4 = (bf16[2,2,128,128]{3,2,1,0:T(8,128)(2,1)}, bf16[2,2,128,128]{3,2,1,0:T(8,128)(2,1)S(1)}, u32[]{:S(2)}) copy-start(bf16[2,2,128,128]{3,2,1,0:T(8,128)(2,1)S(1)} %get-tuple-element.458) | copy-start | bytes 393220 | tf_op jit(solution)/shard_map/while
  353.9 14.6 %copy-start.2 = (bf16[2,2,128,128]{3,2,0,1:T(8,128)(2,1)}, bf16[2,2,128,128]{3,2,0,1:T(8,128)(2,1)S(1)}, u32[]{:S(2)}) copy-start(bf16[2,2,128,128]{3,2,0,1:T(8,128)(2,1)S(1)} %get-tuple-element.457) | copy-start | bytes 393220 | tf_op jit(solution)/shard_map/while
  353.9 14.6 %copy-start.4 = (bf16[2,2,128,128]{3,2,1,0:T(8,128)(2,1)}, bf16[2,2,128,128]{3,2,1,0:T(8,128)(2,1)S(1)}, u32[]{:S(2)}) copy-start(bf16[2,2,128,128]{3,2,1,0:T(8,128)(2,1)S(1)} %get-tuple-element.458) | copy-start | bytes 393220 | tf_op jit(solution)/shard_map/while
  382.3 17.4 %collective-permute-start.18 = (f32[2,2,64,384]{3,2,1,0:T(8,128)S(1)}, f32[2,2,64,384]{3,2,1,0:T(8,128)}, u32[]{:S(2)}, u32[]{:S(2)}) collective-permute-start(f32[2,2,64,384]{3,2,1,0:T(8,128)S(1)} %get-tuple-element.277), channel_id=1, source_target_pairs={{0,8},{8,16},{16,24},{1,9},{9,17},{17,25},{2,10},{10,18},{18,26},{... | collective-permute-start | bytes 1179656 | tf_op jit(solution)/shard_map/ppermute | solution.py:29
  398.4 3.7 collective-permute-start.19
  404.3 30.2 %copy-start.7 = (f32[2,2,64,384]{2,3,1,0:T(8,128)S(1)}, f32[2,2,64,384]{2,3,1,0:T(8,128)}, u32[]{:S(2)}) copy-start(f32[2,2,64,384]{2,3,1,0:T(8,128)} %copy.141) | copy-start | bytes 1179652
  405.8 19.1 %collective-permute-start.20 = (f32[2,2,512,64]{2,3,1,0:T(8,128)S(1)}, f32[2,2,512,64]{2,3,1,0:T(8,128)S(1)}, u32[]{:S(2)}, u32[]{:S(2)}) collective-permute-start(f32[2,2,512,64]{2,3,1,0:T(8,128)S(1)} %get-tuple-element.275), channel_id=1, source_target_pairs={{0,1},{1,2},{2,3},{3,4},{4,5},{5,6},{6,7},{8,9},{9,10},{10,11},{11... | collective-permute-start | bytes 1572872 | tf_op jit(solution)/shard_map/ppermute | solution.py:29
  407.7 27.9 %copy-start.11 = (pred[256]{0:T(512)(128)(4,1)S(1)}, pred[256]{0:T(512)(128)(4,1)}, u32[]{:S(2)}) copy-start(pred[256]{0:T(512)(128)(4,1)} %constant.111.clone.1) | copy-start | bytes 772
  407.7 26.8 %collective-permute-start.21 = (f32[2,2,512,64]{2,3,1,0:T(8,128)S(1)}, f32[2,2,512,64]{2,3,1,0:T(8,128)S(1)}, u32[]{:S(2)}, u32[]{:S(2)}) collective-permute-start(f32[2,2,512,64]{2,3,1,0:T(8,128)S(1)} %get-tuple-element.276), channel_id=1, source_target_pairs={{1,0},{2,1},{3,2},{4,3},{5,4},{6,5},{7,6},{9,8},{10,9},{11,10},{12... | collective-permute-start | bytes 1572872 | tf_op jit(solution)/shard_map/ppermute | solution.py:30
  (65 other events, 467.1 us)
where the time goes:
time: 442 us; the launch traced here: 438 us
  other arithmetic  113 us (26%)
  local copies, waits for them, and re-layouts  98 us (22%)
  matrix products  77.3 us (17%)
  loops' own time  56.5 us (13%)
  starting transfers between devices  54.1 us (12%)
  waiting for transfers between devices  38.9 us (9%)
    dot_general x48, matrix products, apply_right(): jnp.einsum('nrpq,rtqs->ntps', field, table, preferred_element_type=jnp.fl...  73.5 us
    another operation x1, loops' own time, local(): lax.scan(visit, jnp.zeros(extended.shape, jnp.float32), (held, held_detai...  56.5 us
    another operation x37, other arithmetic  46.5 us
    dynamic_update_slice x12, local copies, waits for them, and re-layouts, visit(): return (lax.dynamic_update_slice(carry, current + grads, corner), None)  29.4 us
    ppermute x4, starting transfers between devices, padded(): before = lax.ppermute(last, axis, up)  21.3 us
    ppermute x14, starting transfers between devices, shifted(): return lax.ppermute(block, axis, route)  20.7 us
    mul x12, other arithmetic, pattern_grad(): resid = (far * (valid * (1.0 - ratio))).astype(jnp.bfloat16)  18.1 us
    mul x24, local copies, waits for them, and re-layouts, cmul(): a_re * b_re - a_im * b_im  14.9 us
  transfers between devices with their start and end apart: 22, of which 5 were waited for; matrix products, arithmetic and copies ran while one was open for 4% of the time, Pallas kernels for 0%

commit v1 on v0

v1 whole, which is shorter than its diff:
```python
import functools
import math

import jax
import jax.numpy as jnp
import numpy as np
from jax import lax
from jax.experimental import pallas as pl
from jax.experimental.pallas import tpu as pltpu
from jax.sharding import PartitionSpec as P

FRESNEL = 24.0
REACH_OFFSETS = (-3, -2, -1, 1, 2, 3, 4)
CAP = 2
LANES = 128
NOTE = 16
VMEM_BYTES = 40 * 1024 * 1024


def make_tables(width):
    idx = np.arange(width)
    angle = (idx[:, None] * idx[None, :] % width).astype(np.float32) * np.float32(2.0 * math.pi / width)
    scale = np.float32(1.0 / math.sqrt(width))
    f_re = np.cos(angle) * scale
    f_im = -np.sin(angle) * scale
    centred = (idx + width // 2) % width - width // 2
    theta = (centred * centred).astype(np.float32) * np.float32(math.pi * FRESNEL / (width * width))
    d_re = np.cos(theta)
    d_im = -np.sin(theta)
    m_re = d_re[:, None] * f_re - d_im[:, None] * f_im
    m_im = d_re[:, None] * f_im + d_im[:, None] * f_re
    k_re = f_re @ m_re + f_im @ m_im
    k_im = f_re @ m_im - f_im @ m_re
    tables = []
    for re, im in ((k_re, k_im), (f_re, f_im)):
        tables.append(np.block([[re, -im], [im, re]]))
        tables.append(np.block([[re, im], [-im, re]]))
    return jnp.asarray(np.stack(tables).astype(jnp.bfloat16))


def partners(ncols):
    if ncols == 8:
        return [[i ^ k for i in range(ncols)] for k in (4, 6, 5, 7, 2, 3, 1)]
    return [[(i + k) % ncols for i in range(ncols)] for k in REACH_OFFSETS]


def pack_kernel(kinds, count, owners, at_rows, at_cols, dests, obj, amps, *outs):
    msgs, (left, right, upper, lower) = outs[:kinds], outs[kinds:]
    rows, cols = obj.shape[1:]
    border = amps.shape[1] // 2
    lane = lax.broadcasted_iota(jnp.int32, (1, LANES), 1)
    low = lane < border
    for pair in range(2):
        even, odd = 2 * pair, 2 * pair + 1
        left[pair] = jnp.where(
            low, obj[even, :, :LANES], pltpu.roll(obj[odd, :, :LANES], border, 1)
        ).astype(jnp.bfloat16)
        right[pair] = jnp.where(
            low, pltpu.roll(obj[even, :, cols - LANES :], border, 1), obj[odd, :, cols - LANES :]
        ).astype(jnp.bfloat16)
    for plane in range(4):
        for block in range(cols // LANES):
            span = slice(block * LANES, (block + 1) * LANES)
            upper[plane, block] = obj[plane, :border, span].astype(jnp.bfloat16)
            lower[plane, block] = obj[plane, rows - border :, span].astype(jnp.bfloat16)
    width = amps.shape[1]
    row_id = lax.broadcasted_iota(jnp.int32, (NOTE, LANES), 0)
    lane_id = lax.broadcasted_iota(jnp.int32, (NOTE, LANES), 1)
    for kind in range(kinds):
        found = jnp.int32(0)
        slots = [jnp.int32(0)] * CAP
        for j in range(count):
            mine = owners[j] == dests[kind]
            for slot in range(CAP):
                slots[slot] = jnp.where(mine & (found == slot), j, slots[slot])
            found = found + mine.astype(jnp.int32)
        note = jnp.zeros((NOTE, LANES), jnp.float32)
        for slot in range(CAP):
            j = slots[slot]
            msgs[kind][slot * width : (slot + 1) * width] = amps[j]
            live = (found > slot).astype(jnp.int32)
            for place, value in enumerate((at_rows[j], at_cols[j], live)):
                here = (row_id == slot) & (lane_id == place)
                note = jnp.where(here, value.astype(jnp.float32), note)
        msgs[kind][CAP * width :] = note.astype(jnp.bfloat16)


def unpack_sides(pair, from_right, from_left, border):
    lane = lax.broadcasted_iota(jnp.int32, (1, LANES), 1)
    low = lane < border
    near = from_right[pair].astype(jnp.float32)
    far = from_left[pair].astype(jnp.float32)
    even = jnp.where(low, near, pltpu.roll(far, border, 1))
    odd = jnp.where(low, pltpu.roll(near, border, 1), far)
    return even, odd


def rows_kernel(from_right, from_left, upper, lower, up, down):
    border = upper.shape[2]
    rows = from_right.shape[1]
    blocks = upper.shape[1]
    up[:, :blocks] = upper[...]
    down[:, :blocks] = lower[...]
    for message, at in ((up, 0), (down, rows - border)):
        for pair in range(2):
            even, odd = unpack_sides(
                pair, from_right.at[:, at : at + border], from_left.at[:, at : at + border], border
            )
            message[2 * pair, blocks] = even.astype(jnp.bfloat16)
            message[2 * pair + 1, blocks] = odd.astype(jnp.bfloat16)


def matmul(first, second):
    return jnp.dot(first, second, preferred_element_type=jnp.float32)


def quarters(field):
    half = field.shape[0] // 2
    return field[:half, :half], field[:half, half:], field[half:, :half], field[half:, half:]


def joined(a, b, c, d):
    return jnp.concatenate(
        [jnp.concatenate([a, b], axis=1), jnp.concatenate([c, d], axis=1)], axis=0
    ).astype(jnp.bfloat16)


def swapped(field):
    a, b, c, d = quarters(field)
    return joined(a, c, b, d)


def main_kernel(kinds, tables, probe, obj, from_right, from_left, from_above, from_below, *refs):
    msgs = refs[:kinds]
    centre, up, down = refs[kinds : kinds + 3]
    ext, grad, amps, notes, notes_s, order, sem = refs[kinds + 3 :]
    rows, cols = obj.shape[1:]
    width = probe.shape[2]
    border = width // 2
    blocks = cols // LANES
    span = cols + 2 * border

    for kind in range(kinds):
        note = msgs[kind][CAP * width :].astype(jnp.float32).astype(jnp.int32)
        notes[kind * 8 : (kind + 1) * 8] = note[:8]
    copy = pltpu.make_async_copy(notes, notes_s, sem)
    copy.start()
    for kind in range(kinds):
        for slot in range(CAP):
            amps[kind * CAP + slot] = msgs[kind][slot * width : (slot + 1) * width]
    for plane in range(4):
        for block in range(blocks):
            ext[plane, block, border : border + rows] = obj[plane, :, block * LANES : (block + 1) * LANES]
        for block in range(blocks + 1):
            ext[plane, block, :border] = from_above[plane, block].astype(jnp.float32)
            ext[plane, block, border + rows :] = from_below[plane, block].astype(jnp.float32)
    for pair in range(2):
        even, odd = unpack_sides(pair, from_right, from_left, border)
        ext[2 * pair, blocks, border : border + rows] = even
        ext[2 * pair + 1, blocks, border : border + rows] = odd
    grad[...] = jnp.zeros_like(grad)
    copy.wait()

    total = jnp.int32(0)
    for kind in range(kinds):
        for slot in range(CAP):
            order[total] = kind * CAP + slot
            total = total + notes_s[kind * 8 + slot, 2]
    order[total] = 0

    lane = lax.broadcasted_iota(jnp.int32, (1, LANES), 1)

    def stages(items):
        places = []
        for number in items:
            which = order[number]
            kind, slot = which // CAP, which % CAP
            row = notes_s[kind * 8 + slot, 0]
            col = notes_s[kind * 8 + slot, 1]
            start = col + (span - border)
            start = jnp.where(start >= span, start - span, start)
            first = start // LANES
            shift = start % LANES
            second = jnp.where(first == blocks, 0, first + 1)
            places.append((which, row, first, second, shift))
        windows = []
        for which, row, first, second, shift in places:
            window = []
            for plane in range(4):
                a = ext[plane, first, pl.ds(row, width), :]
                b = ext[plane, second, pl.ds(row, width), :]
                both = jnp.where(lane >= shift, a, b)
                window.append(pltpu.roll(both, (LANES - shift) % LANES, 1))
            windows.append(window)
        fields = []
        for window in windows:
            parts = []
            for mode in range(2):
                p_re, p_im = probe[mode, 0], probe[mode, 1]
                parts.append((p_re * window[0] - p_im * window[1], p_re * window[1] + p_im * window[0]))
            fields.append(joined(parts[0][0], parts[1][0], parts[0][1], parts[1][1]))
        fields = [swapped(matmul(tables[0], f)) for f in fields]
        phis = [matmul(f, tables[1]) for f in fields]
        fields = []
        for window, phi in zip(windows, phis):
            a_re, a_im, b_re, b_im = quarters(phi)
            w_re, w_im = window[2], window[3]
            fields.append(
                joined(
                    a_re * w_re - a_im * w_im,
                    b_re * w_re - b_im * w_im,
                    a_re * w_im + a_im * w_re,
                    b_re * w_im + b_im * w_re,
                )
            )
        fields = [swapped(matmul(tables[2], f)) for f in fields]
        fars = [matmul(f, tables[3]) for f in fields]
        fields = []
        for place, far in zip(places, fars):
            a_re, a_im, b_re, b_im = quarters(far)
            inten = a_re * a_re + a_im * a_im + b_re * b_re + b_im * b_im
            keep = 1.0 - amps[place[0]].astype(jnp.float32) * lax.rsqrt(jnp.maximum(inten, 1.0))
            fields.append(joined(a_re * keep, b_re * keep, a_im * keep, b_im * keep))
        fields = [swapped(matmul(tables[3], f)) for f in fields]
        seconds = [matmul(f, tables[2]) for f in fields]
        fields = []
        for window, second in zip(windows, seconds):
            a_re, a_im, b_re, b_im = quarters(second)
            w_re, w_im = window[2], window[3]
            fields.append(
                joined(
                    w_re * a_re + w_im * a_im,
                    w_re * b_re + w_im * b_im,
                    w_re * a_im - w_im * a_re,
                    w_re * b_im - w_im * b_re,
                )
            )
        fields = [swapped(matmul(tables[1], f)) for f in fields]
        firsts = [matmul(f, tables[0]) for f in fields]
        for number, place, phi, one, two in zip(items, places, phis, firsts, seconds):
            _, row, first, second, shift = place
            sums = []
            probes = (probe[0, 0], probe[0, 1], probe[1, 0], probe[1, 1])
            for left, right in ((probes, one), (quarters(phi), two)):
                p_re, p_im, q_re, q_im = left
                a_re, a_im, b_re, b_im = quarters(right)
                sums.append(p_re * a_re + p_im * a_im + q_re * b_re + q_im * b_im)
                sums.append(p_re * a_im - p_im * a_re + q_re * b_im - q_im * b_re)
            live = number < total
            for plane in range(4):
                moved = pltpu.roll(sums[plane], shift, 1)
                grad[plane, first, pl.ds(row, width), :] += jnp.where((lane >= shift) & live, moved, 0.0)
                grad[plane, second, pl.ds(row, width), :] += jnp.where((lane < shift) & live, moved, 0.0)

    def visit(step, carry):
        stages((2 * step, 2 * step + 1))
        return carry

    lax.fori_loop(0, (total + 1) // 2, visit, 0)

    for plane in range(4):
        for block in range(blocks + 1):
            centre[plane, block] = grad[plane, block, border : border + rows]
            up[plane, block] = grad[plane, block, :border].astype(jnp.bfloat16)
            down[plane, block] = grad[plane, block, border + rows :].astype(jnp.bfloat16)


def sides_kernel(centre, from_above, from_below, middle, right, left):
    blocks = centre.shape[1] - 1
    rows = centre.shape[2]
    border = from_above.shape[2]
    lane = lax.broadcasted_iota(jnp.int32, (1, LANES), 1)
    low = lane < border

    def total(plane, block):
        whole = centre[plane, block]
        top = whole[:border] + from_above[plane, block].astype(jnp.float32)
        bottom = whole[rows - border :] + from_below[plane, block].astype(jnp.float32)
        return jnp.concatenate([top, whole[border : rows - border], bottom], axis=0)

    for pair in range(2):
        even, odd = total(2 * pair, blocks), total(2 * pair + 1, blocks)
        right[pair] = jnp.where(low, even, pltpu.roll(odd, border, 1)).astype(jnp.bfloat16)
        left[pair] = jnp.where(low, pltpu.roll(even, border, 1), odd).astype(jnp.bfloat16)
    for plane in range(4):
        for block in range(blocks):
            middle[plane, :, block * LANES : (block + 1) * LANES] = total(plane, block)


def final_kernel(middle, from_right, from_left, out):
    cols = middle.shape[2]
    border = LANES // 2
    lane = lax.broadcasted_iota(jnp.int32, (1, LANES), 1)
    low = lane < border
    for pair in range(2):
        near = from_left[pair].astype(jnp.float32)
        far = from_right[pair].astype(jnp.float32)
        even, odd = 2 * pair, 2 * pair + 1
        for plane, first, last in (
            (even, near, pltpu.roll(far, border, 1)),
            (odd, pltpu.roll(near, border, 1), far),
        ):
            add_first = jnp.where(low, first, 0.0)
            add_last = jnp.where(low, 0.0, last)
            if cols == LANES:
                out[plane] = middle[plane] + add_first + add_last
                continue
            out[plane, :, :LANES] = middle[plane, :, :LANES] + add_first
            if cols > 2 * LANES:
                out[plane, :, LANES : cols - LANES] = middle[plane, :, LANES : cols - LANES]
            out[plane, :, cols - LANES :] = middle[plane, :, cols - LANES :] + add_last


def local(ncols, nrows, objects, probe, amplitudes, owners, off_rows, off_cols):
    width = amplitudes.shape[-1]
    border = width // 2
    count = amplitudes.shape[2]
    rows, cols = objects.shape[2:]
    blocks = cols // LANES
    routes = partners(ncols)
    kinds = len(routes)
    myself = lax.axis_index("col")
    dests = jnp.asarray(np.array(routes, np.int32))[:, myself]
    obj = objects.reshape(4, rows, cols)
    vmem = pl.BlockSpec(memory_space=pltpu.VMEM)
    smem = pl.BlockSpec(memory_space=pltpu.SMEM)
    params = pltpu.CompilerParams(vmem_limit_bytes=VMEM_BYTES)
    bf16 = functools.partial(jax.ShapeDtypeStruct, dtype=jnp.bfloat16)
    f32 = functools.partial(jax.ShapeDtypeStruct, dtype=jnp.float32)

    def ahead(array, axis, size, step):
        return lax.ppermute(array, axis, [(i, i + step) for i in range(size) if 0 <= i + step < size])

    packed = pl.pallas_call(
        functools.partial(pack_kernel, kinds, count),
        out_shape=[bf16((CAP * width + NOTE, LANES))] * kinds
        + [bf16((2, rows, LANES))] * 2
        + [bf16((4, blocks, border, LANES))] * 2,
        in_specs=[smem] * 4 + [vmem] * 2,
        out_specs=[vmem] * (kinds + 4),
        compiler_params=params,
        name="pack",
    )(
        owners.reshape(count),
        off_rows.reshape(count),
        off_cols.reshape(count),
        dests,
        obj,
        amplitudes.reshape(count, width, width),
    )
    left, right, upper, lower = packed[kinds:]
    from_right = ahead(left, "col", ncols, -1)
    from_left = ahead(right, "col", ncols, 1)
    msgs = [
        lax.ppermute(msg, "col", list(enumerate(route)))
        for msg, route in zip(packed[:kinds], routes)
    ]
    up, down = pl.pallas_call(
        rows_kernel,
        out_shape=[bf16((4, blocks + 1, border, LANES))] * 2,
        in_specs=[vmem] * 4,
        out_specs=[vmem] * 2,
        compiler_params=params,
        name="rows",
    )(from_right, from_left, upper, lower)
    from_below = ahead(up, "row", nrows, -1)
    from_above = ahead(down, "row", nrows, 1)

    centre, up, down = pl.pallas_call(
        functools.partial(main_kernel, kinds),
        out_shape=[f32((4, blocks + 1, rows, LANES))] + [bf16((4, blocks + 1, border, LANES))] * 2,
        in_specs=[vmem] * (7 + kinds),
        out_specs=[vmem] * 3,
        scratch_shapes=[
            pltpu.VMEM((4, blocks + 1, rows + 2 * border, LANES), jnp.float32),
            pltpu.VMEM((4, blocks + 1, rows + 2 * border, LANES), jnp.float32),
            pltpu.VMEM((kinds * CAP, width, width), jnp.bfloat16),
            pltpu.VMEM((kinds * 8, LANES), jnp.int32),
            pltpu.SMEM((kinds * 8, LANES), jnp.int32),
            pltpu.SMEM((kinds * CAP + 1,), jnp.int32),
            pltpu.SemaphoreType.DMA,
        ],
        compiler_params=params,
        name="gradients",
    )(make_tables(width), probe, obj, from_right, from_left, from_above, from_below, *msgs)

    back_below = ahead(up, "row", nrows, -1)
    back_above = ahead(down, "row", nrows, 1)
    middle, right, left = pl.pallas_call(
        sides_kernel,
        out_shape=[f32((4, rows, cols))] + [bf16((2, rows, LANES))] * 2,
        in_specs=[vmem] * 3,
        out_specs=[vmem] * 3,
        compiler_params=params,
        name="sides",
    )(centre, back_above, back_below)
    back_left = ahead(right, "col", ncols, 1)
    back_right = ahead(left, "col", ncols, -1)
    out = pl.pallas_call(
        final_kernel,
        out_shape=f32((4, rows, cols)),
        in_specs=[vmem] * 3,
        out_specs=vmem,
        compiler_params=params,
        name="final",
    )(middle, back_right, back_left)
    return out.reshape(objects.shape)


def solution(mesh):
    placed = (
        P(None, None, "row", "col"),
        P(),
        P("row", "col", None, None, None),
        P("row", "col", None),
        P("row", "col", None),
        P("row", "col", None),
    )
    return jax.shard_map(
        functools.partial(local, mesh.shape["col"], mesh.shape["row"]),
        mesh=mesh,
        in_specs=placed,
        out_specs=P(None, None, "row", "col"),
        check_vma=False,
    )
```

time: 442 us -> 74.1 us (0.17)
  the two profiles are of different devices: /device:TPU:8 before, /device:TPU:25 now
where the time goes in v1:
time: 74.1 us; the launch traced here: 73.7 us
  starting transfers between devices  36.1 us (49%)
  waiting for transfers between devices  20.9 us (28%)
  Pallas kernels  10.8 us (15%)
  local copies, waits for them, and re-layouts  5.76 us (8%)
    ppermute x8, starting transfers between devices, ahead(): lax.ppermute(array, axis, [(i, i + step) for i in range(size) if 0 <= i +...  25.9 us
    ppermute x8, waiting for transfers between devices, ahead(): lax.ppermute(array, axis, [(i, i + step) for i in range(size) if 0 <= i +...  17 us
    ppermute x7, starting transfers between devices, local(): lax.ppermute(msg, 'col', list(enumerate(route)))  10.2 us
    pallas_call x1, Pallas kernels, local(): pl.pallas_call(functools.partial(main_kernel, kinds), out_shape=[f32((4,...  8.64 us
    unnamed x16, local copies, waits for them, and re-layouts  5.07 us
    ppermute x7, waiting for transfers between devices, local(): lax.ppermute(msg, 'col', list(enumerate(route)))  3.88 us
  transfers between devices with their start and end apart: 15, of which 9 were waited for; matrix products, arithmetic and copies ran while one was open for 0% of the time, Pallas kernels for 0%

profile of v1, /device:TPU:25, one launch (start us, length us, event | category | flops | bytes accessed | tf_op | source)
XLA Modules:
  0.0 73.7 jit_solution(291872663078707795)
XLA Ops:
  0.0 0.7 dynamic-slice_bitcast_fusion.dests
  0.7 0.0 copy-start
  0.7 1.2 %copy-done = f32[2,2,256,256]{3,2,1,0:T(8,128)S(1)} copy-done((f32[2,2,256,256]{3,2,1,0:T(8,128)S(1)}, f32[2,2,256,256]{3,2,1,0:T(8,128)}, u32[]{:S(2)}) %copy-start) | copy-done | bytes 1048600
  1.9 0.0 copy-start.4
  1.9 0.9 %copy-done.4 = bf16[1,1,6,128,128]{4,3,2,1,0:T(8,128)(2,1)S(1)} copy-done((bf16[1,1,6,128,128]{4,3,2,1,0:T(8,128)(2,1)S(1)}, bf16[1,1,6,128,128]{4,3,2,1,0:T(8,128)(2,1)}, u32[]{:S(2)}) %copy-start.4) | copy-done | bytes 196632
  2.8 0.0 copy-start.5
  2.8 0.7 copy-done.5
  3.5 0.7 copy-done.6
  4.2 0.7 copy-done.7
  4.8 0.8 %pack.1 = (bf16[272,128]{1,0:T(8,128)(2,1)S(1)}, bf16[272,128]{1,0:T(8,128)(2,1)S(1)}, bf16[272,128]{1,0:T(8,128)(2,1)S(1)}, bf16[272,128]{1,0:T(8,128)(2,1)S(1)...) custom-call(s32[6]{0:T(128)S(1)} %bitcast.11, ...), custom_call_target="tpu_custom_call" | custom-call | tf_op jit(solution)/shard_map/pack/pallas_call | solution.py:334
  5.6 3.0 %collective-permute-start = (bf16[2,256,128]{2,1,0:T(8,128)(2,1)S(1)}, bf16[2,256,128]{2,1,0:T(8,128)(2,1)S(1)}, u32[]{:S(2)}, u32[]{:S(2)}) collective-permute-start(bf16[2,256,128]{2,1,0:T(8,128)(2,1)S(1)} %get-tuple-element.24), channel_id=1, source_target_pairs={{1,0},{2,1},{3,2},{4,3},{5,4},{6,5},{7,6},{9,8},{10,9},{11,10},{12... | collective-permute-start | bytes 393224 | tf_op jit(solution)/shard_map/ppermute | solution.py:332
  8.6 2.3 %collective-permute-start.1 = (bf16[2,256,128]{2,1,0:T(8,128)(2,1)S(1)}, bf16[2,256,128]{2,1,0:T(8,128)(2,1)S(1)}, u32[]{:S(2)}, u32[]{:S(2)}) collective-permute-start(bf16[2,256,128]{2,1,0:T(8,128)(2,1)S(1)} %get-tuple-element.25), channel_id=1, source_target_pairs={{0,1},{1,2},{2,3},{3,4},{4,5},{5,6},{6,7},{8,9},{9,10},{10,11},{11... | collective-permute-start | bytes 393224 | tf_op jit(solution)/shard_map/ppermute | solution.py:332
  10.9 0.1 collective-permute-start.4
  11.0 0.8 %collective-permute-done.from_right = bf16[2,256,128]{2,1,0:T(8,128)(2,1)S(1)} collective-permute-done((bf16[2,256,128]{2,1,0:T(8,128)(2,1)S(1)}, bf16[2,256,128]{2,1,0:T(8,128)(2,1)S(1)}, u32[]{:S(2)}, u32[]{:S(2)}) %collective-permute-start) | collective-permute-done | bytes 131104 | tf_op jit(solution)/shard_map/ppermute | solution.py:332
  11.8 3.5 %collective-permute-done.1.from_left = bf16[2,256,128]{2,1,0:T(8,128)(2,1)S(1)} collective-permute-done((bf16[2,256,128]{2,1,0:T(8,128)(2,1)S(1)}, bf16[2,256,128]{2,1,0:T(8,128)(2,1)S(1)}, u32[]{:S(2)}, u32[]{:S(2)}) %collective-permute-start.1) | collective-permute-done | bytes 131104 | tf_op jit(solution)/shard_map/ppermute | solution.py:332
  15.4 0.1 rows.1
  15.5 5.7 %collective-permute-start.2 = (bf16[4,3,64,128]{3,2,1,0:T(8,128)(2,1)S(1)}, bf16[4,3,64,128]{3,2,1,0:T(8,128)(2,1)S(1)}, u32[]{:S(2)}, u32[]{:S(2)}) collective-permute-start(bf16[4,3,64,128]{3,2,1,0:T(8,128)(2,1)S(1)} %get-tuple-element.28), channel_id=1, source_target_pairs={{0,8},{8,16},{16,24},{1,9},{9,17},{17,25},{2,10},{10,18},{18,26},{... | collective-permute-start | bytes 589832 | tf_op jit(solution)/shard_map/ppermute | solution.py:332
  21.2 1.9 %collective-permute-start.3 = (bf16[4,3,64,128]{3,2,1,0:T(8,128)(2,1)S(1)}, bf16[4,3,64,128]{3,2,1,0:T(8,128)(2,1)S(1)}, u32[]{:S(2)}, u32[]{:S(2)}) collective-permute-start(bf16[4,3,64,128]{3,2,1,0:T(8,128)(2,1)S(1)} %get-tuple-element.29), channel_id=1, source_target_pairs={{8,0},{16,8},{24,16},{9,1},{17,9},{25,17},{10,2},{18,10},{26,18},{... | collective-permute-start | bytes 589832 | tf_op jit(solution)/shard_map/ppermute | solution.py:332
  23.1 0.1 collective-permute-start.5
  23.2 1.3 %collective-permute-start.6 = (bf16[272,128]{1,0:T(8,128)(2,1)S(1)}, bf16[272,128]{1,0:T(8,128)(2,1)S(1)}, u32[]{:S(2)}, u32[]{:S(2)}) collective-permute-start(bf16[272,128]{1,0:T(8,128)(2,1)S(1)} %get-tuple-element.32), channel_id=1, source_target_pairs={{0,5},{1,4},{2,7},{3,6},{4,1},{5,0},{6,3},{7,2},{8,13},{9,12},{10,... | collective-permute-start | bytes 208904 | tf_op jit(solution)/shard_map/ppermute | solution.py:355
  24.5 0.0 collective-permute-done.4.refs_0_
  24.5 3.4 %collective-permute-start.7 = (bf16[272,128]{1,0:T(8,128)(2,1)S(1)}, bf16[272,128]{1,0:T(8,128)(2,1)S(1)}, u32[]{:S(2)}, u32[]{:S(2)}) collective-permute-start(bf16[272,128]{1,0:T(8,128)(2,1)S(1)} %get-tuple-element.33), channel_id=1, source_target_pairs={{0,7},{1,6},{2,5},{3,4},{4,3},{5,2},{6,1},{7,0},{8,15},{9,14},{10,... | collective-permute-start | bytes 208904 | tf_op jit(solution)/shard_map/ppermute | solution.py:355
  27.9 0.5 collective-permute-done.5.refs_1_
  28.5 3.0 %collective-permute-start.8 = (bf16[272,128]{1,0:T(8,128)(2,1)S(1)}, bf16[272,128]{1,0:T(8,128)(2,1)S(1)}, u32[]{:S(2)}, u32[]{:S(2)}) collective-permute-start(bf16[272,128]{1,0:T(8,128)(2,1)S(1)} %get-tuple-element.34), channel_id=1, source_target_pairs={{0,2},{1,3},{2,0},{3,1},{4,6},{5,7},{6,4},{7,5},{8,10},{9,11},{10,... | collective-permute-start | bytes 208904 | tf_op jit(solution)/shard_map/ppermute | solution.py:355
  31.5 0.6 collective-permute-done.6.refs_2_
  32.1 0.0 collective-permute-start.9
  32.1 0.0 collective-permute-done.7.refs_3_
  32.1 2.2 %collective-permute-start.10 = (bf16[272,128]{1,0:T(8,128)(2,1)S(1)}, bf16[272,128]{1,0:T(8,128)(2,1)S(1)}, u32[]{:S(2)}, u32[]{:S(2)}) collective-permute-start(bf16[272,128]{1,0:T(8,128)(2,1)S(1)} %get-tuple-element.36), channel_id=1, source_target_pairs={{0,1},{1,0},{2,3},{3,2},{4,5},{5,4},{6,7},{7,6},{8,9},{9,8},{10,11... | collective-permute-start | bytes 208904 | tf_op jit(solution)/shard_map/ppermute | solution.py:355
  34.3 0.0 collective-permute-done.8.refs_4_
  34.3 1.9 %collective-permute-done.9.refs_5_ = bf16[272,128]{1,0:T(8,128)(2,1)S(1)} collective-permute-done((bf16[272,128]{1,0:T(8,128)(2,1)S(1)}, bf16[272,128]{1,0:T(8,128)(2,1)S(1)}, u32[]{:S(2)}, u32[]{:S(2)}) %collective-permute-start.9) | collective-permute-done | bytes 69664 | tf_op jit(solution)/shard_map/ppermute | solution.py:355
  36.2 0.8 %collective-permute-done.10.refs_6_ = bf16[272,128]{1,0:T(8,128)(2,1)S(1)} collective-permute-done((bf16[272,128]{1,0:T(8,128)(2,1)S(1)}, bf16[272,128]{1,0:T(8,128)(2,1)S(1)}, u32[]{:S(2)}, u32[]{:S(2)}) %collective-permute-start.10) | collective-permute-done | bytes 69664 | tf_op jit(solution)/shard_map/ppermute | solution.py:355
  37.1 0.0 collective-permute-done.2.from_above
  37.1 0.0 collective-permute-done.3.from_below
  37.1 0.0 copy-done.1
  37.1 0.0 copy-done.2
  37.1 0.0 copy-start.3
  37.1 0.9 %copy-done.3 = f32[2,2,128,128]{3,2,1,0:T(8,128)S(1)} copy-done((f32[2,2,128,128]{3,2,1,0:T(8,128)S(1)}, f32[2,2,128,128]{3,2,1,0:T(8,128)}, u32[]{:S(2)}) %copy-start.3) | copy-done | bytes 262168
  38.1 8.6 %gradients.1 = (f32[4,3,256,128]{3,2,1,0:T(8,128)S(1)}, bf16[4,3,64,128]{3,2,1,0:T(8,128)(2,1)S(1)}, bf16[4,3,64,128]{3,2,1,0:T(8,128)(2,1)S(1)}) custom-call(bf16[4,256,256]{2,1,0:T(8,128)(2,1)S(1)} %copy-done.2, f32[2,2,128,128]{3,2,1,0:T(8,128)S(1)} %copy-done.3, f32[4,256,256]{2,1,0:T(8,128)S(1)} %bitcast.9, ...), custom_call_target="tpu_custom_call" | custom-call | tf_op jit(solution)/shard_map/gradients/pallas_call | solution.py:369
  46.7 3.4 %collective-permute-start.11 = (bf16[4,3,64,128]{3,2,1,0:T(8,128)(2,1)S(1)}, bf16[4,3,64,128]{3,2,1,0:T(8,128)(2,1)S(1)}, u32[]{:S(2)}, u32[]{:S(2)}) collective-permute-start(bf16[4,3,64,128]{3,2,1,0:T(8,128)(2,1)S(1)} %get-tuple-element.38), channel_id=1, source_target_pairs={{0,8},{8,16},{16,24},{1,9},{9,17},{17,25},{2,10},{10,18},{18,26},{... | collective-permute-start | bytes 589832 | tf_op jit(solution)/shard_map/ppermute | solution.py:332
  50.2 1.9 %collective-permute-start.12 = (bf16[4,3,64,128]{3,2,1,0:T(8,128)(2,1)S(1)}, bf16[4,3,64,128]{3,2,1,0:T(8,128)(2,1)S(1)}, u32[]{:S(2)}, u32[]{:S(2)}) collective-permute-start(bf16[4,3,64,128]{3,2,1,0:T(8,128)(2,1)S(1)} %get-tuple-element.39), channel_id=1, source_target_pairs={{8,0},{16,8},{24,16},{9,1},{17,9},{25,17},{10,2},{18,10},{26,18},{... | collective-permute-start | bytes 589832 | tf_op jit(solution)/shard_map/ppermute | solution.py:332
  52.1 0.7 collective-permute-done.11.from_above
  52.7 4.4 %collective-permute-done.12.from_below = bf16[4,3,64,128]{3,2,1,0:T(8,128)(2,1)S(1)} collective-permute-done((bf16[4,3,64,128]{3,2,1,0:T(8,128)(2,1)S(1)}, bf16[4,3,64,128]{3,2,1,0:T(8,128)(2,1)S(1)}, u32[]{:S(2)}, u32[]{:S(2)}) %collective-permute-start.12) | collective-permute-done | bytes 196640 | tf_op jit(solution)/shard_map/ppermute | solution.py:332
  57.1 0.2 sides.1
  57.3 5.7 %collective-permute-start.13 = (bf16[2,256,128]{2,1,0:T(8,128)(2,1)S(1)}, bf16[2,256,128]{2,1,0:T(8,128)(2,1)S(1)}, u32[]{:S(2)}, u32[]{:S(2)}) collective-permute-start(bf16[2,256,128]{2,1,0:T(8,128)(2,1)S(1)} %get-tuple-element.41), channel_id=1, source_target_pairs={{1,0},{2,1},{3,2},{4,3},{5,4},{6,5},{7,6},{9,8},{10,9},{11,10},{12... | collective-permute-start | bytes 393224 | tf_op jit(solution)/shard_map/ppermute | solution.py:332
  63.1 1.9 %collective-permute-start.14 = (bf16[2,256,128]{2,1,0:T(8,128)(2,1)S(1)}, bf16[2,256,128]{2,1,0:T(8,128)(2,1)S(1)}, u32[]{:S(2)}, u32[]{:S(2)}) collective-permute-start(bf16[2,256,128]{2,1,0:T(8,128)(2,1)S(1)} %get-tuple-element.42), channel_id=1, source_target_pairs={{0,1},{1,2},{2,3},{3,4},{4,5},{5,6},{6,7},{8,9},{9,10},{10,11},{11... | collective-permute-start | bytes 393224 | tf_op jit(solution)/shard_map/ppermute | solution.py:332
  65.0 0.0 collective-permute-done.13.from_right
  65.0 7.6 %collective-permute-done.14.from_left = bf16[2,256,128]{2,1,0:T(8,128)(2,1)S(1)} collective-permute-done((bf16[2,256,128]{2,1,0:T(8,128)(2,1)S(1)}, bf16[2,256,128]{2,1,0:T(8,128)(2,1)S(1)}, u32[]{:S(2)}, u32[]{:S(2)}) %collective-permute-start.14) | collective-permute-done | bytes 131104 | tf_op jit(solution)/shard_map/ppermute | solution.py:332
  72.6 1.1 %final.1 = f32[4,256,256]{2,1,0:T(8,128)} custom-call(f32[4,256,256]{2,1,0:T(8,128)S(1)} %get-tuple-element.40.middle, bf16[2,256,128]{2,1,0:T(8,128)(2,1)S(1)} %collective-permute-done.13.from_right, bf16[2,256,128]{2,1,0:T(8,128)(2,1)S(1)} %collective-permute-done.14.from_left), custom_call_target="tpu_custom_call" | custom-call | tf_op jit(solution)/shard_map/final/pallas_call | solution.py:399
  (4 shorter events, 0.0 us)
Async XLA Ops:
  0.7 1.2 %copy-start = (f32[2,2,256,256]{3,2,1,0:T(8,128)S(1)}, f32[2,2,256,256]{3,2,1,0:T(8,128)}, u32[]{:S(2)}) copy-start(f32[2,2,256,256]{3,2,1,0:T(8,128)} %param.8) | copy-start | bytes 3145732
  1.9 0.9 %copy-start.4 = (bf16[1,1,6,128,128]{4,3,2,1,0:T(8,128)(2,1)S(1)}, bf16[1,1,6,128,128]{4,3,2,1,0:T(8,128)(2,1)}, u32[]{:S(2)}) copy-start(bf16[1,1,6,128,128]{4,3,2,1,0:T(8,128)(2,1)} %param.10) | copy-start | bytes 589828
  2.8 0.7 copy-start.5
  3.5 0.7 copy-start.6
  4.2 0.7 copy-start.7
  4.8 32.3 %copy-start.1 = (f32[2,2,256,256]{3,2,1,0:T(8,128)S(1)}, f32[2,2,256,256]{3,2,1,0:T(8,128)}, u32[]{:S(2)}) copy-start(f32[2,2,256,256]{3,2,1,0:T(8,128)} %param.8) | copy-start | bytes 3145732
  4.8 32.3 %copy-start.2 = (bf16[4,256,256]{2,1,0:T(8,128)(2,1)S(1)}, bf16[4,256,256]{2,1,0:T(8,128)(2,1)}, u32[]{:S(2)}) copy-start(bf16[4,256,256]{2,1,0:T(8,128)(2,1)} %constant.13.clone.tables) | copy-start | bytes 1572868
  5.6 6.3 %collective-permute-start = (bf16[2,256,128]{2,1,0:T(8,128)(2,1)S(1)}, bf16[2,256,128]{2,1,0:T(8,128)(2,1)S(1)}, u32[]{:S(2)}, u32[]{:S(2)}) collective-permute-start(bf16[2,256,128]{2,1,0:T(8,128)(2,1)S(1)} %get-tuple-element.24), channel_id=1, source_target_pairs={{1,0},{2,1},{3,2},{4,3},{5,4},{6,5},{7,6},{9,8},{10,9},{11,10},{12... | collective-permute-start | bytes 393224 | tf_op jit(solution)/shard_map/ppermute | solution.py:332
  8.6 6.8 %collective-permute-start.1 = (bf16[2,256,128]{2,1,0:T(8,128)(2,1)S(1)}, bf16[2,256,128]{2,1,0:T(8,128)(2,1)S(1)}, u32[]{:S(2)}, u32[]{:S(2)}) collective-permute-start(bf16[2,256,128]{2,1,0:T(8,128)(2,1)S(1)} %get-tuple-element.25), channel_id=1, source_target_pairs={{0,1},{1,2},{2,3},{3,4},{4,5},{5,6},{6,7},{8,9},{9,10},{10,11},{11... | collective-permute-start | bytes 393224 | tf_op jit(solution)/shard_map/ppermute | solution.py:332
  10.9 13.6 %collective-permute-start.4 = (bf16[272,128]{1,0:T(8,128)(2,1)S(1)}, bf16[272,128]{1,0:T(8,128)(2,1)S(1)}, u32[]{:S(2)}, u32[]{:S(2)}) collective-permute-start(bf16[272,128]{1,0:T(8,128)(2,1)S(1)} %get-tuple-element.30), channel_id=1, source_target_pairs={{0,4},{1,5},{2,6},{3,7},{4,0},{5,1},{6,2},{7,3},{8,12},{9,13},{10,... | collective-permute-start | bytes 208904 | tf_op jit(solution)/shard_map/ppermute | solution.py:355
  15.5 21.6 %collective-permute-start.2 = (bf16[4,3,64,128]{3,2,1,0:T(8,128)(2,1)S(1)}, bf16[4,3,64,128]{3,2,1,0:T(8,128)(2,1)S(1)}, u32[]{:S(2)}, u32[]{:S(2)}) collective-permute-start(bf16[4,3,64,128]{3,2,1,0:T(8,128)(2,1)S(1)} %get-tuple-element.28), channel_id=1, source_target_pairs={{0,8},{8,16},{16,24},{1,9},{9,17},{17,25},{2,10},{10,18},{18,26},{... | collective-permute-start | bytes 589832 | tf_op jit(solution)/shard_map/ppermute | solution.py:332
  21.2 15.9 %collective-permute-start.3 = (bf16[4,3,64,128]{3,2,1,0:T(8,128)(2,1)S(1)}, bf16[4,3,64,128]{3,2,1,0:T(8,128)(2,1)S(1)}, u32[]{:S(2)}, u32[]{:S(2)}) collective-permute-start(bf16[4,3,64,128]{3,2,1,0:T(8,128)(2,1)S(1)} %get-tuple-element.29), channel_id=1, source_target_pairs={{8,0},{16,8},{24,16},{9,1},{17,9},{25,17},{10,2},{18,10},{26,18},{... | collective-permute-start | bytes 589832 | tf_op jit(solution)/shard_map/ppermute | solution.py:332
  23.1 5.3 %collective-permute-start.5 = (bf16[272,128]{1,0:T(8,128)(2,1)S(1)}, bf16[272,128]{1,0:T(8,128)(2,1)S(1)}, u32[]{:S(2)}, u32[]{:S(2)}) collective-permute-start(bf16[272,128]{1,0:T(8,128)(2,1)S(1)} %get-tuple-element.31), channel_id=1, source_target_pairs={{0,6},{1,7},{2,4},{3,5},{4,2},{5,3},{6,0},{7,1},{8,14},{9,15},{10,... | collective-permute-start | bytes 208904 | tf_op jit(solution)/shard_map/ppermute | solution.py:355
  23.2 8.9 %collective-permute-start.6 = (bf16[272,128]{1,0:T(8,128)(2,1)S(1)}, bf16[272,128]{1,0:T(8,128)(2,1)S(1)}, u32[]{:S(2)}, u32[]{:S(2)}) collective-permute-start(bf16[272,128]{1,0:T(8,128)(2,1)S(1)} %get-tuple-element.32), channel_id=1, source_target_pairs={{0,5},{1,4},{2,7},{3,6},{4,1},{5,0},{6,3},{7,2},{8,13},{9,12},{10,... | collective-permute-start | bytes 208904 | tf_op jit(solution)/shard_map/ppermute | solution.py:355
  24.5 7.5 %collective-permute-start.7 = (bf16[272,128]{1,0:T(8,128)(2,1)S(1)}, bf16[272,128]{1,0:T(8,128)(2,1)S(1)}, u32[]{:S(2)}, u32[]{:S(2)}) collective-permute-start(bf16[272,128]{1,0:T(8,128)(2,1)S(1)} %get-tuple-element.33), channel_id=1, source_target_pairs={{0,7},{1,6},{2,5},{3,4},{4,3},{5,2},{6,1},{7,0},{8,15},{9,14},{10,... | collective-permute-start | bytes 208904 | tf_op jit(solution)/shard_map/ppermute | solution.py:355
  28.5 5.9 %collective-permute-start.8 = (bf16[272,128]{1,0:T(8,128)(2,1)S(1)}, bf16[272,128]{1,0:T(8,128)(2,1)S(1)}, u32[]{:S(2)}, u32[]{:S(2)}) collective-permute-start(bf16[272,128]{1,0:T(8,128)(2,1)S(1)} %get-tuple-element.34), channel_id=1, source_target_pairs={{0,2},{1,3},{2,0},{3,1},{4,6},{5,7},{6,4},{7,5},{8,10},{9,11},{10,... | collective-permute-start | bytes 208904 | tf_op jit(solution)/shard_map/ppermute | solution.py:355
  32.1 4.2 %collective-permute-start.9 = (bf16[272,128]{1,0:T(8,128)(2,1)S(1)}, bf16[272,128]{1,0:T(8,128)(2,1)S(1)}, u32[]{:S(2)}, u32[]{:S(2)}) collective-permute-start(bf16[272,128]{1,0:T(8,128)(2,1)S(1)} %get-tuple-element.35), channel_id=1, source_target_pairs={{0,3},{1,2},{2,1},{3,0},{4,7},{5,6},{6,5},{7,4},{8,11},{9,10},{10,... | collective-permute-start | bytes 208904 | tf_op jit(solution)/shard_map/ppermute | solution.py:355
  32.1 5.0 %collective-permute-start.10 = (bf16[272,128]{1,0:T(8,128)(2,1)S(1)}, bf16[272,128]{1,0:T(8,128)(2,1)S(1)}, u32[]{:S(2)}, u32[]{:S(2)}) collective-permute-start(bf16[272,128]{1,0:T(8,128)(2,1)S(1)} %get-tuple-element.36), channel_id=1, source_target_pairs={{0,1},{1,0},{2,3},{3,2},{4,5},{5,4},{6,7},{7,6},{8,9},{9,8},{10,11... | collective-permute-start | bytes 208904 | tf_op jit(solution)/shard_map/ppermute | solution.py:355
  37.1 1.0 %copy-start.3 = (f32[2,2,128,128]{3,2,1,0:T(8,128)S(1)}, f32[2,2,128,128]{3,2,1,0:T(8,128)}, u32[]{:S(2)}) copy-start(f32[2,2,128,128]{3,2,1,0:T(8,128)} %probe.1) | copy-start | bytes 786436
  46.7 6.0 %collective-permute-start.11 = (bf16[4,3,64,128]{3,2,1,0:T(8,128)(2,1)S(1)}, bf16[4,3,64,128]{3,2,1,0:T(8,128)(2,1)S(1)}, u32[]{:S(2)}, u32[]{:S(2)}) collective-permute-start(bf16[4,3,64,128]{3,2,1,0:T(8,128)(2,1)S(1)} %get-tuple-element.38), channel_id=1, source_target_pairs={{0,8},{8,16},{16,24},{1,9},{9,17},{17,25},{2,10},{10,18},{18,26},{... | collective-permute-start | bytes 589832 | tf_op jit(solution)/shard_map/ppermute | solution.py:332
  50.2 7.0 %collective-permute-start.12 = (bf16[4,3,64,128]{3,2,1,0:T(8,128)(2,1)S(1)}, bf16[4,3,64,128]{3,2,1,0:T(8,128)(2,1)S(1)}, u32[]{:S(2)}, u32[]{:S(2)}) collective-permute-start(bf16[4,3,64,128]{3,2,1,0:T(8,128)(2,1)S(1)} %get-tuple-element.39), channel_id=1, source_target_pairs={{8,0},{16,8},{24,16},{9,1},{17,9},{25,17},{10,2},{18,10},{26,18},{... | collective-permute-start | bytes 589832 | tf_op jit(solution)/shard_map/ppermute | solution.py:332
  57.3 7.7 %collective-permute-start.13 = (bf16[2,256,128]{2,1,0:T(8,128)(2,1)S(1)}, bf16[2,256,128]{2,1,0:T(8,128)(2,1)S(1)}, u32[]{:S(2)}, u32[]{:S(2)}) collective-permute-start(bf16[2,256,128]{2,1,0:T(8,128)(2,1)S(1)} %get-tuple-element.41), channel_id=1, source_target_pairs={{1,0},{2,1},{3,2},{4,3},{5,4},{6,5},{7,6},{9,8},{10,9},{11,10},{12... | collective-permute-start | bytes 393224 | tf_op jit(solution)/shard_map/ppermute | solution.py:332
  63.1 9.5 %collective-permute-start.14 = (bf16[2,256,128]{2,1,0:T(8,128)(2,1)S(1)}, bf16[2,256,128]{2,1,0:T(8,128)(2,1)S(1)}, u32[]{:S(2)}, u32[]{:S(2)}) collective-permute-start(bf16[2,256,128]{2,1,0:T(8,128)(2,1)S(1)} %get-tuple-element.42), channel_id=1, source_target_pairs={{0,1},{1,2},{2,3},{3,4},{4,5},{5,6},{6,7},{8,9},{9,10},{10,11},{11... | collective-permute-start | bytes 393224 | tf_op jit(solution)/shard_map/ppermute | solution.py:332
